TPU v7x, 128 devices: a whole 4x4x4 slice. The times are simulated.
128 devices in a mesh: bx: 16 (over z_hi, x, core), by: 8 (over z_lo, y).
Axes of the slice: x: 4, y: 4, z: 4 (z_hi: 2, z_lo: 2; z = z_hi * 2 + z_lo), core: 2. Of those that a mesh axis runs over, the one named last changes fastest.
Arguments:
- spectra: bfloat16 [16384, 10, 2, 256], P(('bx', 'by')), may hold values from -220 to 220, as said below
- band_edges: int32 [9], replicated, may hold values from 0 to 256, as said below
Outputs:
- stacked: float32 [16384, 6, 2, 8, 128], P(('bx', 'by'))
Inputs may be any that keep to these rules, and one draw needn't show every extreme that they name: `spectra`: values of moderate size for every channel, window and bin. `band_edges`: Rising; the first entry is 0, the last is 256, and each band holds at least 16 bins.
All inputs are finite; a program needn't handle non-finite values.
Results may differ from a plain program's by a relative error of at most 0.0003.
Values may be sent and summed in bfloat16 or wider, within the bound.
A program may use at most 128 MiB of HBM per device.

v0:
```python
import functools
import jax
import jax.numpy as jnp
from jax import lax
from jax.experimental import pallas as pl
from jax.experimental.pallas import tpu as pltpu
from jax.sharding import PartitionSpec as P

ROUNDS = 6
EPS = 1e-06
MESH = pl.DeviceIdType.MESH
AHEAD = 2
COMPUTE = True
COMM = True


def flip(index, bit):
    return index + bit - 2 * bit * ((index // bit) % 2)


def band_mask(edges_ref, bands, nbins):
    row = lax.broadcasted_iota(jnp.int32, (bands, nbins), 0)
    freq = lax.broadcasted_iota(jnp.int32, (bands, nbins), 1)
    low = jnp.zeros((bands, nbins), jnp.int32)
    high = jnp.zeros((bands, nbins), jnp.int32)
    for b in range(bands):
        low = jnp.where(row == b, edges_ref[b], low)
        high = jnp.where(row == b, edges_ref[b + 1], high)
    return jnp.where((freq >= low) & (freq < high), 1.0, 0.0).astype(jnp.float32)


def kernel(count, edges_ref, x_ref, acc_ref, norm_ref,
           xv, own, got, hop_a, hop_b, left, spread, power, parts,
           load_sem, send_sem, recv_sem, psend_sem, precv_sem):
    channels, windows, nparts, nbins = xv.shape
    bands = norm_ref.shape[0]
    bx, by = lax.axis_index("bx"), lax.axis_index("by")
    core = (flip(bx, 1), by)
    x1 = (flip(bx, 2), by)
    x3 = (flip(flip(bx, 2), 4), by)
    z1 = (bx, flip(by, 4))
    z3 = (flip(bx, 8), flip(by, 4))
    y1 = (bx, flip(by, 1))
    y3 = (bx, flip(flip(by, 1), 2))

    load = pltpu.make_async_copy(x_ref, xv, load_sem)
    load.start()

    barrier = pltpu.get_barrier_semaphore()
    neighbours = (core, x1, x3, z1, z3, y1, y3)
    for device in neighbours:
        pl.semaphore_signal(barrier, inc=1, device_id=device, device_id_type=MESH)

    def remote(stream, c, src, dst, device):
        return pltpu.make_async_remote_copy(
            src_ref=src, dst_ref=dst, send_sem=send_sem.at[stream, c],
            recv_sem=recv_sem.at[stream, c], device_id=device, device_id_type=MESH)

    half = pl.ds(0, channels), pl.ds(channels, channels)
    def copy(stream, c):
        if stream == 0:
            return remote(0, c, got.at[4, c], got.at[0, c], z3)
        if stream == 1:
            return remote(1, c, got.at[2, c], got.at[1, c], x3)
        if stream == 2:
            return remote(2, c, own.at[c], got.at[2, c], x1)
        if stream == 3:
            return remote(3, c, own.at[c], got.at[3, c], core)
        if stream == 4:
            return remote(4, c, own.at[c], got.at[4, c], z1)
        if stream == 5:
            return remote(5, c, hop_a.at[c], got.at[5, c, half[0]], y3)
        if stream == 6:
            return remote(6, c, own.at[c, half[0]], hop_a.at[c], y1)
        if stream == 7:
            return remote(7, c, own.at[c, half[1]], hop_b.at[c], y3)
        return remote(8, c, hop_b.at[c], got.at[5, c, half[1]], y1)

    rows = nparts * channels
    def prepare(c):
        block = xv[:, c].reshape(rows, nbins)
        r = lax.broadcasted_iota(jnp.int32, (rows, rows), 0)
        k = lax.broadcasted_iota(jnp.int32, (rows, rows), 1)
        pick = jnp.where(k == nparts * (r % channels) + r // channels, 1.0, 0.0).astype(jnp.bfloat16)
        own[c] = jnp.dot(pick, block, preferred_element_type=jnp.float32).astype(jnp.bfloat16)

    def send(c):
        for stream in (2, 4, 6, 7, 3):
            copy(stream, c).start()

    load.wait()
    prepare(0)
    pl.semaphore_wait(barrier, len(neighbours))
    if COMM: send(0)
    for c in range(1, AHEAD):
        prepare(c)
        if COMM: send(c)
    @pl.loop(AHEAD, windows)
    def _(c):
        prepare(c)

    mask = band_mask(edges_ref, bands, nbins)
    er = lax.broadcasted_iota(jnp.int32, spread.shape, 0)
    ek = lax.broadcasted_iota(jnp.int32, spread.shape, 1)
    spread[...] = jnp.where(ek == er // bands, 1.0, 0.0).astype(jnp.bfloat16)

    def squares(c, total):
        v = own[c].astype(jnp.float32)
        return total + jnp.sum((v * v).reshape(rows // 8, 8, nbins), axis=0)
    bins = lax.fori_loop(0, windows, squares, jnp.zeros((8, nbins), jnp.float32))
    bins = jnp.sum(bins, axis=0, keepdims=True)
    power[...] = jnp.broadcast_to(jnp.sum(mask * bins, axis=1, keepdims=True), power.shape)

    route = (core, x1, x3, z1, z3, y1, y3)
    def exchange(step):
        return pltpu.make_async_remote_copy(
            src_ref=parts.at[step], dst_ref=parts.at[len(route) + step], send_sem=psend_sem.at[step],
            recv_sem=precv_sem.at[step], device_id=route[step], device_id_type=MESH)

    def begin(step):
        parts[step] = power[...]
        exchange(step).start()

    def end(step):
        exchange(step).wait_recv()
        power[...] += parts[len(route) + step]

    begin(0)

    acc_ref[...] = jnp.zeros_like(acc_ref)

    def build(c):
        for p in range(nparts):
            wide = jnp.dot(spread[...], own[c, half[p]], preferred_element_type=jnp.float32)
            wide = wide.reshape(channels, bands, nbins) * mask[None]
            left[c, :, p * nbins:(p + 1) * nbins] = wide.reshape(channels * bands, nbins).astype(jnp.bfloat16)

    def accumulate(r, c):
        if not COMPUTE: return
        cos, sin = got[r, c, half[0]], got[r, c, half[1]]
        right = jnp.concatenate(
            [jnp.concatenate([cos, sin], axis=1), jnp.concatenate([-sin, cos], axis=1)], axis=0)
        acc_ref[r] += lax.dot_general(
            left[c], right, (((1,), (1,)), ((), ())), preferred_element_type=jnp.float32)

    def wait(stream, c):
        if COMM: copy(stream, c).wait_recv()

    def start(stream, c):
        if COMM: copy(stream, c).start()

    @pl.loop(0, windows)
    def _(c):
        if COMM:
            @pl.when(c + AHEAD < windows)
            def _():
                send(c + AHEAD)
        if COMPUTE: build(c)
        wait(2, c)
        start(1, c)
        wait(4, c)
        start(0, c)
        wait(6, c)
        start(5, c)
        wait(7, c)
        start(8, c)
        for step in range(len(route)):
            @pl.when(c == step + 1)
            def _(step=step):
                end(step)
                if step + 1 < len(route):
                    begin(step + 1)
        wait(3, c)
        accumulate(3, c)
        accumulate(2, c)
        accumulate(4, c)

        @pl.when(c > 0)
        def _():
            for r in (1, 0, 5):
                wait(r, c - 1)
                if r == 5:
                    wait(8, c - 1)
                accumulate(r, c - 1)

    for r in (1, 0, 5):
        wait(r, windows - 1)
        if r == 5:
            wait(8, windows - 1)
        accumulate(r, windows - 1)

    norm_ref[...] = 1.0 / (power[...] / (count * windows) + EPS)
    if COMM:
        @pl.loop(0, windows)
        def _(c):
            for stream in range(9):
                copy(stream, c).wait_send()
    for step in range(len(route)):
        exchange(step).wait_send()


def finish(acc_ref, norm_ref, out_ref):
    norm = norm_ref[...]
    for r in range(ROUNDS):
        for p in range(2):
            lanes = norm.shape[1]
            block = acc_ref[r, :, p * lanes:(p + 1) * lanes]
            out_ref[:, r, p] = block.reshape(-1, *norm.shape) * norm[None]


def body(spectra, band_edges):
    channels, windows, parts, nbins = spectra.shape
    bands = band_edges.shape[0] - 1
    devices = lax.axis_size("bx") * lax.axis_size("by")
    rows = channels * parts
    dma = pltpu.SemaphoreType.DMA
    vmem = pltpu.VMEM
    acc, norm = pl.pallas_call(
        functools.partial(kernel, channels * devices),
        out_shape=(vmem((ROUNDS, channels * bands, parts * channels), jnp.float32),
                   vmem((bands, 128), jnp.float32)),
        in_specs=[pl.BlockSpec(memory_space=pltpu.SMEM), pl.BlockSpec(memory_space=pl.ANY)],
        out_specs=(pl.BlockSpec(memory_space=vmem), pl.BlockSpec(memory_space=vmem)),
        scratch_shapes=[
            vmem(spectra.shape, jnp.bfloat16),
            vmem((windows, rows, nbins), jnp.bfloat16),
            vmem((ROUNDS, windows, rows, nbins), jnp.bfloat16),
            vmem((windows, channels, nbins), jnp.bfloat16),
            vmem((windows, channels, nbins), jnp.bfloat16),
            vmem((windows, channels * bands, parts * nbins), jnp.bfloat16),
            vmem((channels * bands, channels), jnp.bfloat16),
            vmem((bands, 128), jnp.float32),
            vmem((14, bands, 128), jnp.float32),
            dma(()), dma((9, windows)), dma((9, windows)), dma((7,)), dma((7,)),
        ],
        compiler_params=pltpu.CompilerParams(
            collective_id=0, has_side_effects=True, vmem_limit_bytes=48 * 2**20),
        name="exchange",
    )(band_edges, spectra)
    tile = 16
    return pl.pallas_call(
        finish,
        grid=(channels // tile,),
        out_shape=jax.ShapeDtypeStruct((channels, ROUNDS, parts, bands, channels), jnp.float32),
        in_specs=[pl.BlockSpec((ROUNDS, tile * bands, parts * channels), lambda i: (0, i, 0)),
                  pl.BlockSpec((bands, 128), lambda i: (0, 0))],
        out_specs=pl.BlockSpec((tile, ROUNDS, parts, bands, channels), lambda i: (i, 0, 0, 0, 0)),
        name="finish",
    )(acc, norm)


def solution(mesh):
    return jax.shard_map(
        body,
        mesh=mesh,
        in_specs=(P(("bx", "by"), None, None, None), P()),
        out_specs=P(("bx", "by"), None, None, None, None),
        check_vma=False,
    )
```

profile of v0, /device:TPU:0, one launch (start us, length us, event | category | flops | bytes accessed | tf_op | source)
XLA Modules:
  0.0 68.7 jit_solution(6483376737124894223)
XLA Ops:
  0.0 57.5 %exchange.1 = (f32[6,1024,256]{2,1,0:T(8,128)S(1)}, f32[8,128]{1,0:T(8,128)S(1)}) custom-call(s32[9]{0:T(128)} %edges_ref.1, bf16[128,10,2,256]{3,2,1,0:T(2,128)(2,1)} %x_ref.1), custom_call_target="tpu_custom_call" | custom-call | tf_op jit(solution)/shard_map/exchange/pallas_call | solution.py:218
  57.5 0.0 copy-start
  57.5 2.6 %copy-done = f32[6,1024,256]{2,1,0:T(8,128)} copy-done((f32[6,1024,256]{2,1,0:T(8,128)}, f32[6,1024,256]{2,1,0:T(8,128)S(1)}, u32[]{:S(2)}) %copy-start) | copy-done | bytes 6291480
  60.1 0.0 copy-start.1
  60.1 0.6 copy-done.1
  60.7 7.9 %finish.1 = f32[128,6,2,8,128]{4,3,2,1,0:T(8,128)} custom-call(f32[6,1024,256]{2,1,0:T(8,128)} %copy-done, f32[8,128]{1,0:T(8,128)} %copy-done.1), custom_call_target="tpu_custom_call" | custom-call | tf_op jit(solution)/shard_map/finish/pallas_call | solution.py:241
Async XLA Ops:
  57.5 2.6 %copy-start = (f32[6,1024,256]{2,1,0:T(8,128)}, f32[6,1024,256]{2,1,0:T(8,128)S(1)}, u32[]{:S(2)}) copy-start(f32[6,1024,256]{2,1,0:T(8,128)S(1)} %get-tuple-element.7.acc_ref) | copy-start | bytes 18874372
  60.1 0.6 copy-start.1
where the time goes:
time: 69 us; the launch traced here: 68.7 us
  Pallas kernels  65.4 us (95%)
  local copies, waits for them, and re-layouts  3.22 us (5%)
    pallas_call x1, Pallas kernels, body(): pl.pallas_call(functools.partial(kernel, channels * devices), out_shape=(...  57.5 us
    pallas_call x1, Pallas kernels, body(): pl.pallas_call(finish, grid=(channels // tile,), out_shape=jax.ShapeDtype...  7.95 us
    unnamed x4, local copies, waits for them, and re-layouts  3.22 us

commit v1 on v0

--- a/solution.py
+++ b/solution.py
@@ -201,10 +201,12 @@
 
 def finish(acc_ref, norm_ref, out_ref):
     norm = norm_ref[...]
+    size = out_ref.shape[0] * norm.shape[0]
+    rows = pl.ds(pl.multiple_of(pl.program_id(0) * size, size), size)
     for r in range(ROUNDS):
         for p in range(2):
             lanes = norm.shape[1]
-            block = acc_ref[r, :, p * lanes:(p + 1) * lanes]
+            block = acc_ref[r, rows, p * lanes:(p + 1) * lanes]
             out_ref[:, r, p] = block.reshape(-1, *norm.shape) * norm[None]
 
 
@@ -242,11 +244,11 @@
         finish,
         grid=(channels // tile,),
         out_shape=jax.ShapeDtypeStruct((channels, ROUNDS, parts, bands, channels), jnp.float32),
-        in_specs=[pl.BlockSpec((ROUNDS, tile * bands, parts * channels), lambda i: (0, i, 0)),
-                  pl.BlockSpec((bands, 128), lambda i: (0, 0))],
+        in_specs=[pl.BlockSpec(memory_space=vmem), pl.BlockSpec(memory_space=vmem)],
         out_specs=pl.BlockSpec((tile, ROUNDS, parts, bands, channels), lambda i: (i, 0, 0, 0, 0)),
+        compiler_params=pltpu.CompilerParams(vmem_limit_bytes=16 * 2**20),
         name="finish",
-    )(acc, norm)
+    )(*(pltpu.with_memory_space_constraint(v, vmem) for v in (acc, norm)))
 
 
 def solution(mesh):

time: 69 us -> 61.7 us (0.89)
  Pallas kernels: 65.4 us -> 61.6 us
  local copies, waits for them, and re-layouts: 3.22 us -> 0 us
    pallas_call x1, Pallas kernels: 7.95 us -> 4.11 us  [body(): pl.pallas_call(finish, grid=(channels // tile,), out_shape=jax.ShapeDtype...]
    unnamed x4 -> x0, local copies, waits for them, and re-layouts: 3.22 us -> none
where the time goes in v1:
time: 61.7 us; the launch traced here: 61.6 us
  Pallas kernels  61.6 us (100%)
    pallas_call x1, Pallas kernels, body(): pl.pallas_call(functools.partial(kernel, channels * devices), out_shape=(...  57.5 us
    pallas_call x1, Pallas kernels, body(): pl.pallas_call(finish, grid=(channels // tile,), out_shape=jax.ShapeDtype...  4.11 us

profile of v1, /device:TPU:0, one launch (start us, length us, event | category | flops | bytes accessed | tf_op | source)
XLA Modules:
  0.0 61.6 jit_solution(7586875010729446469)
XLA Ops:
  0.0 57.5 %exchange.1 = (f32[6,1024,256]{2,1,0:T(8,128)S(1)}, f32[8,128]{1,0:T(8,128)S(1)}) custom-call(s32[9]{0:T(128)} %edges_ref.1, bf16[128,10,2,256]{3,2,1,0:T(2,128)(2,1)} %x_ref.1), custom_call_target="tpu_custom_call" | custom-call | tf_op jit(solution)/shard_map/exchange/pallas_call | solution.py:220
  57.5 4.1 %finish.1 = f32[128,6,2,8,128]{4,3,2,1,0:T(8,128)} custom-call(f32[6,1024,256]{2,1,0:T(8,128)S(1)} %get-tuple-element.7.acc_ref, f32[8,128]{1,0:T(8,128)S(1)} %get-tuple-element.8.norm_ref), custom_call_target="tpu_custom_call" | custom-call | tf_op jit(solution)/shard_map/finish/pallas_call | solution.py:243
